TPU v7x, 32 devices: a whole 2x2x4 slice. The times are simulated.
32 devices in a mesh: group: 2 (over x), dp: 8 (over z, y), fsdp: 2 (over core).
Axes of the slice: x: 2, y: 2, z: 4, core: 2. Of those that a mesh axis runs over, the one named last changes fastest.
Arguments:
- image_tokens: bfloat16 [256, 64, 1536], P(('group', 'dp', 'fsdp')), parts along dimension 0, may hold values from -6 to 6
- text_features: bfloat16 [256, 1536], P(('group', 'dp', 'fsdp')), parts along dimension 0, may hold values from -6 to 6
- kv_weight: bfloat16 [2, 1536, 1536], P(None, None, 'fsdp'), may hold values from -0.15625 to 0.15625
- head_weight: bfloat16 [2, 1536, 1536], P(None, 'fsdp'), may hold values from -0.15625 to 0.15625
- probe: float32 [1536], replicated, may hold values from -5 to 5
- scale_key: float32 [1536], replicated, may hold values from 0.25 to 1.75
- scale_value: float32 [1536], replicated, may hold values from 0.25 to 1.75
- scale_text: float32 [1536], replicated, may hold values from 0.25 to 1.75
Outputs:
- image_grad: bfloat16 [256, 1536], P(('group', 'dp', 'fsdp')), parts along dimension 0
- text_grad: bfloat16 [256, 1536], P(('group', 'dp', 'fsdp')), parts along dimension 0
- ia3_grad: float32 [6, 1536], P('group'), parts along dimension 0
There are 2 independent parts, one for each index of `group`. A program takes and returns all parts, laid end to end along the dimension named above; an argument that names none is the same for every part. Nothing has to cross between parts.
All inputs are finite; a program needn't handle non-finite values.
Results may differ from a plain program's by a relative error of at most 0.0058.
Values may be sent and summed in bfloat16 or wider, within the bound.
A program may use at most 128 MiB of HBM per device.

v0:
```python
import math

import jax
import jax.numpy as jnp
from jax import lax
from jax.sharding import PartitionSpec as P

D = 1536
HEADS = 16
HEAD_SIZE = 96
PATCHES = 64


LOGIT_SCALE = 10.0
LOGIT_BIAS = -2.0
EPSILON = 1e-06
HIGHEST = lax.Precision.HIGHEST


def unit_norm(embedding):
    inverse = lax.rsqrt(jnp.sum(embedding * embedding, axis=-1, keepdims=True) + EPSILON)
    return (embedding * inverse, inverse)


def unit_back(unit_vec, inverse, upstream):
    return inverse * (upstream - unit_vec * jnp.sum(unit_vec * upstream, axis=-1, keepdims=True))


def pair_coeffs(image_sent, text_block, diagonal):
    logits = (
        LOGIT_SCALE
        * lax.dot_general(
            image_sent, text_block, (((1,), (1,)), ((), ())), preferred_element_type=jnp.float32
        )
        + LOGIT_BIAS
    )
    return (jax.nn.sigmoid(logits) - diagonal).astype(jnp.bfloat16)


def image_side(coeffs, text_block):
    return LOGIT_SCALE * jnp.dot(coeffs, text_block, preferred_element_type=jnp.float32)


def text_side(coeffs, image_sent):
    return LOGIT_SCALE * lax.dot_general(
        coeffs, image_sent, (((0,), (0,)), ((), ())), preferred_element_type=jnp.float32
    )


def pool_heads(keys_raw, values_raw, key_gain, probe_heads):
    image_count = keys_raw.shape[0]
    scaled_keys = keys_raw * key_gain
    scores = jnp.einsum("nphe,he->nhp", scaled_keys, probe_heads, precision=HIGHEST) / math.sqrt(
        HEAD_SIZE
    )
    attention = jax.nn.softmax(scores, axis=-1)
    pooled_raw = jnp.einsum("nhp,nphe->nhe", attention, values_raw, precision=HIGHEST).reshape(
        image_count, -1
    )
    return (attention, pooled_raw)


def key_grad(attention, d_pooled, keys_raw, values_raw, value_gain, probe_heads):
    image_count, patch_count, head_count, head_width = values_raw.shape
    d_heads = d_pooled.reshape(image_count, head_count, head_width)
    scaled_values = values_raw * value_gain
    d_attention = jnp.einsum("nphe,nhe->nhp", scaled_values, d_heads, precision=HIGHEST)
    d_scores = attention * (d_attention - jnp.sum(attention * d_attention, axis=-1, keepdims=True))
    mixed_keys = jnp.einsum("nhp,nphe->he", d_scores, keys_raw, precision=HIGHEST)
    return (probe_heads * mixed_keys).reshape(-1) / math.sqrt(HEAD_SIZE)


def on_device(
    image_tokens, text_features, kv_weight, head_weight, probe, scale_key, scale_value, scale_text
):
    row_count = image_tokens.shape[0]
    flat_tokens = image_tokens.reshape(row_count * PATCHES, D)
    projected = jnp.einsum(
        "td,kdc->ktc",
        flat_tokens,
        lax.all_gather(kv_weight, "fsdp", axis=2, tiled=True),
        preferred_element_type=jnp.float32,
    )
    full_heads = lax.all_gather(head_weight, "fsdp", axis=1, tiled=True)
    keys_raw = projected[0].reshape(row_count, PATCHES, HEADS, HEAD_SIZE)
    values_raw = projected[1].reshape(row_count, PATCHES, HEADS, HEAD_SIZE)
    value_gain = scale_value.reshape(HEADS, HEAD_SIZE)
    probe_heads = probe.reshape(HEADS, HEAD_SIZE)
    attention, pooled_raw = pool_heads(
        keys_raw, values_raw, scale_key.reshape(HEADS, HEAD_SIZE), probe_heads
    )
    pooled = (pooled_raw * scale_value).astype(jnp.bfloat16)
    image_emb = jnp.dot(pooled, full_heads[0], preferred_element_type=jnp.float32)
    text_raw = jnp.dot(text_features, full_heads[1], preferred_element_type=jnp.float32)
    image_unit, image_inv = unit_norm(image_emb)
    text_unit, text_inv = unit_norm(text_raw * scale_text)
    image_sent = image_unit.astype(jnp.bfloat16)
    text_sent = text_unit.astype(jnp.bfloat16)
    all_text = lax.all_gather(text_sent, ("dp", "fsdp"), axis=0, tiled=True)
    my_index = lax.axis_index(("dp", "fsdp"))
    column_ids = lax.broadcasted_iota(jnp.int32, (row_count, all_text.shape[0]), 1)
    image_ids = (
        lax.broadcasted_iota(jnp.int32, (row_count, all_text.shape[0]), 0) + my_index * row_count
    )
    coeffs = pair_coeffs(image_sent, all_text, (column_ids == image_ids).astype(jnp.float32))
    image_grad = image_side(coeffs, all_text)
    text_grad = lax.psum_scatter(
        text_side(coeffs, image_sent), ("dp", "fsdp"), scatter_dimension=0, tiled=True
    )
    image_back = unit_back(image_unit, image_inv, image_grad).astype(jnp.bfloat16)
    d_pooled = lax.dot_general(
        image_back, full_heads[0], (((1,), (1,)), ((), ())), preferred_element_type=jnp.float32
    )
    grad_value = jnp.sum(d_pooled * pooled_raw, axis=0)
    grad_key = key_grad(attention, d_pooled, keys_raw, values_raw, value_gain, probe_heads)
    text_back = unit_back(text_unit, text_inv, text_grad)
    grad_text = jnp.sum(text_back * text_raw, axis=0)
    totals = lax.psum(jnp.stack([grad_key, grad_value, grad_text]), ("dp", "fsdp"))
    batch_total = row_count * lax.axis_size("dp") * lax.axis_size("fsdp")
    return (image_grad.astype(jnp.bfloat16), text_grad.astype(jnp.bfloat16), totals / batch_total)


def solution(mesh):
    in_specs = (
        P(("group", "dp", "fsdp"), None, None),
        P(("group", "dp", "fsdp"), None),
        P(None, None, "fsdp"),
        P(None, "fsdp", None),
        P(),
        P(),
        P(),
        P(),
    )
    out_specs = (
        P(("group", "dp", "fsdp"), None),
        P(("group", "dp", "fsdp"), None),
        P("group", None),
    )
    return jax.shard_map(
        on_device, mesh=mesh, in_specs=in_specs, out_specs=out_specs, check_vma=False
    )
```

profile of v0, /device:TPU:0, one launch (start us, length us, event | category | flops | bytes accessed | tf_op | source)
XLA Modules:
  0.0 249.3 jit_solution(1539333501015576322)
XLA Ops:
  7.2 0.0 copy-start
  7.2 0.0 all-gather.3.cloned.1.call-start
  7.2 6.8 %copy.15 = bf16[2,1536,768]{1,2,0:T(8,128)(2,1)} copy(bf16[2,1536,768]{2,1,0:T(8,128)(2,1)} %param.10) | data formatting | bytes 9437184 | tf_op args[2]
  14.0 0.0 copy-start.5
  14.0 0.0 copy-start.7
  14.0 0.0 copy-start.8
  14.0 0.0 all-gather.3.cloned.1.call-update
  14.0 0.0 all-gather.5.cloned.1.call-start
  14.1 0.7 all-gather.5.cloned.1.call-update
  14.8 0.0 reduce-scatter.2.cloned.1.call-start
  14.8 0.0 copy-done.5
  14.8 0.1 reshape.63
  14.9 0.1 reshape.59
  15.0 0.0 copy-done.7
  15.0 0.1 mul.132
  15.0 0.0 copy-done.8
  15.0 0.1 mul.135
  15.1 22.0 %all-gather.3.cloned.1.call-done = bf16[2,1536,1536]{1,2,0:T(8,128)(2,1)} async-done(((bf16[2,1536,768]{1,2,0:T(8,128)(2,1)}), bf16[2,1536,1536]{1,2,0:T(8,128)(2,1)}) %all-gather.3.cloned.1.call-update) | async-done | bytes 9437200 | tf_op jit(solution)/shard_map/all_gather | solution.py:81
  37.1 0.0 copy-done
  37.1 7.7 %convolution_bitcast_fusion = f32[2,512,1536]{1,2,0:T(8,128)S(1)} fusion(bf16[2,1536,1536]{1,2,0:T(8,128)(2,1)} %all-gather.3.cloned.1.call-done, bf16[512,1536,1]{1,0,2:T(8,128)(2,1)S(1)} %bitcast.56), kind=kOutput, calls=%fused_computation.4 | convolution fusion | flops 4831838208 | bytes 17301504 | tf_op jit(solution)/shard_map/td,kdc->ktc/dot_general | solution.py:78
  44.8 4.6 %fusion.32 = (f32[1,512,1536]{1,2,0:T(8,128)}, f32[1,512,1536]{1,2,0:T(8,128)}) fusion(f32[2,512,1536]{1,2,0:T(8,128)S(1)} %convolution_bitcast_fusion), kind=kLoop, calls=%fused_computation.61 | loop fusion | bytes 12582912 | tf_op jit(solution)/shard_map/slice | solution.py:85
  49.4 4.1 %copy.16 = f32[1,512,1536]{2,1,0:T(8,128)} copy(f32[1,512,1536]{1,2,0:T(8,128)} %get-tuple-element.3) | data formatting | bytes 6291456 | tf_op jit(solution)/shard_map/slice | solution.py:85
  53.4 5.5 %reshape_squeeze.6 = f32[8,64,16,96]{3,2,1,0:T(8,128)} reshape(f32[1,512,1536]{2,1,0:T(8,128)} %copy.16) | data formatting | bytes 6291456 | tf_op jit(solution)/shard_map/reshape;squeeze | solution.py:85
  59.0 3.5 %copy.17 = f32[1,512,1536]{2,1,0:T(8,128)} copy(f32[1,512,1536]{1,2,0:T(8,128)} %get-tuple-element.4) | data formatting | bytes 6291456 | tf_op jit(solution)/shard_map/slice | solution.py:86
  62.5 5.1 %reshape_squeeze.7 = f32[8,64,16,96]{3,2,1,0:T(8,128)} reshape(f32[1,512,1536]{2,1,0:T(8,128)} %copy.17) | data formatting | bytes 6291456 | tf_op jit(solution)/shard_map/reshape;squeeze | solution.py:86
  67.6 2.5 %broadcast_multiply_fusion.1 = f32[8,64,16,96]{3,2,1,0:T(8,128)S(1)} fusion(f32[8,64,16,96]{3,2,1,0:T(8,128)} %reshape_squeeze.6, f32[16,96]{1,0:T(8,128)S(1)} %mul.132), kind=kLoop, calls=%fused_computation.18 | loop fusion | flops 786432 | bytes 6297600 | tf_op jit(solution)/shard_map/mul | solution.py:52
  70.1 0.0 copy-start.3
  70.1 10.4 %fusion.8 = f32[16,1,8,64]{3,1,2,0:T(1,128)S(1)} fusion(f32[16,96,1,1]{1,2,3,0:T(1,128)S(1)} %bitcast.63, f32[8,64,16,96]{3,2,1,0:T(8,128)S(1)} %broadcast_multiply_fusion.1), kind=kOutput, calls=%fused_computation.11 | convolution fusion | flops 9437184 | bytes 3184640 | tf_op jit(solution)/shard_map/nphe,he->nhp/dot_general | solution.py:53
  80.6 2.8 %fusion.33 = (f32[8,16]{0,1:T(8,128)S(1)}, f32[8,16,64]{2,0,1:T(8,128)S(1)}) fusion(f32[16,8,64]{2,1,0:T(8,128)S(1)} %bitcast.61), kind=kOutput, calls=%fused_computation.62 | output fusion | flops 24639 | bytes 66048 | tf_op jit(solution)/shard_map/sub | solution.py:56
  83.4 0.1 fusion.31
  83.5 0.0 copy-done.3
  83.5 4.4 %fusion.6 = f32[8,16,1,96]{3,2,1,0:T(1,128)S(1)} fusion(f32[8,64,16,96]{3,2,1,0:T(8,128)S(1)} %copy-done.3, f32[8,16,64,1]{2,0,1,3:T(8,128)S(1)} %fusion.31), kind=kOutput, calls=%fused_computation.9 | convolution fusion | flops 9437184 | bytes 3227648 | tf_op jit(solution)/shard_map/nhp,nphe->nhe/dot_general | solution.py:57
  87.9 0.1 reshape.61
  88.0 0.1 convert_element_type.28
  88.1 4.6 %broadcast_multiply_fusion = f32[8,64,16,96]{3,2,1,0:T(8,128)} fusion(f32[8,64,16,96]{3,2,1,0:T(8,128)} %reshape_squeeze.7, f32[16,96]{1,0:T(8,128)S(1)} %mul.135), kind=kLoop, calls=%fused_computation.17 | loop fusion | flops 786432 | bytes 6297600 | tf_op jit(solution)/shard_map/mul | solution.py:66
  92.7 0.0 copy-start.4
  92.7 0.0 copy-start.6
  92.7 0.0 all-gather.5.cloned.1.call-done
  92.7 3.2 %multiply_reduce_fusion.5 = (f32[8]{0:T(128)S(1)}, f32[8,1536]{1,0:T(8,128)S(1)}) fusion(bf16[8,1536]{1,0:T(8,128)(2,1)S(1)} %convert_element_type.28, bf16[2,1536,1536]{2,1,0:T(8,128)(2,1)} %all-gather.5.cloned.1.call-done), kind=kOutput, calls=%fused_computation.44 | convolution fusion | flops 37773304 | bytes 4792352 | tf_op jit(solution)/shard_map/dot_general | solution.py:93
  95.9 0.0 copy-done.4
  95.9 0.0 copy-done.6
  95.9 3.2 %multiply_reduce_fusion.4 = (f32[8]{0:T(128)S(1)}, f32[8,1536]{1,0:T(8,128)S(1)}) fusion(f32[1536]{0:T(1024)S(1)} %copy-done.4, bf16[8,1536]{1,0:T(8,128)(2,1)S(1)} %copy-done.6, bf16[2,1536,1536]{2,1,0:T(8,128)(2,1)} %all-gather.5.cloned.1.call-done), kind=kOutput, calls=%fused_computation.43 | convolution fusion | flops 37785592 | bytes 4798496 | tf_op jit(solution)/shard_map/dot_general | solution.py:94
  99.1 0.1 fusion.26
  99.2 22.7 %all_gather.11 = bf16[128,1536]{1,0:T(8,128)(2,1)S(1)} all-gather(bf16[8,1536]{1,0:T(8,128)(2,1)S(1)} %fusion.26), channel_id=1, replica_groups=mesh['group'=2,'dp'=8,'fsdp'=2] {'dp','fsdp'}, dimensions={0}, use_global_device_ids=true | all-gather | bytes 417792 | tf_op jit(solution)/shard_map/all_gather | solution.py:99
  121.9 0.2 fusion.20
  122.1 0.9 multiply_reduce_fusion.3
  123.0 1.2 convolution_multiply_fusion
  124.3 3.7 %multiply_reduce_fusion.2 = (f32[1536]{0:T(1024)S(1)}, f32[8,1536]{1,0:T(8,128)S(1)}) fusion(f32[8,1536]{1,0:T(8,128)S(1)} %reshape.61, bf16[2,1536,1536]{2,1,0:T(8,128)(2,1)} %all-gather.5.cloned.1.call-done, f32[8,1536]{1,0:T(8,128)S(1)} %get-tuple-element.15, f32[8,1536]{1,0:T(8,128)S(1)} %get-tuple-element.14, f32[8]{0:T(128)S(1)} %get-tuple-element.5, ...), kind=kOutput, calls=%fused_computation.40 | convolution fusion | flops 37833216 | bytes 4921408 | tf_op jit(solution)/shard_map/dot_general | solution.py:111
  127.9 0.1 reshape.67
  128.0 0.0 reduce-scatter.2.cloned.1.call-update
  128.1 0.0 copy-start.2
  128.1 0.0 copy-start.1
  128.1 10.0 %fusion.4 = f32[8,16,1,64]{3,2,1,0:T(1,128)S(1)} fusion(f32[8,16,96,1]{2,3,1,0:T(1,128)S(1)} %bitcast.59, f32[8,64,16,96]{3,2,1,0:T(8,128)} %broadcast_multiply_fusion), kind=kOutput, calls=%fused_computation.7 | convolution fusion | flops 9437184 | bytes 3227648 | tf_op jit(solution)/shard_map/nphe,nhe->nhp/dot_general | solution.py:67
  138.1 0.2 fusion.21
  138.3 0.1 fusion.22
  138.4 0.0 copy-done.2
  138.4 3.9 %fusion.2 = f32[16,1,96,1]{2,1,3,0:T(1,128)S(1)} fusion(f32[8,16,64,1]{2,3,0,1:T(1,128)S(1)} %bitcast.60, f32[8,64,16,96]{3,2,1,0:T(8,128)S(1)} %copy-done.2), kind=kOutput, calls=%fused_computation.5 | convolution fusion | flops 9437184 | bytes 3184640 | tf_op jit(solution)/shard_map/nhp,nphe->he/dot_general | solution.py:69
  142.3 0.1 div.41
  142.4 39.6 %reduce-scatter.2.cloned.1.call-done = f32[8,1536]{1,0:T(8,128)} async-done(((f32[128,1536]{1,0:T(8,128)}), f32[8,1536]{1,0:T(8,128)}) %reduce-scatter.2.cloned.1.call-update) | async-done | bytes 49168 | tf_op jit(solution)/shard_map/reduce_scatter | solution.py:107
  182.0 1.0 multiply_reduce_fusion.1
  183.0 1.5 multiply_reduce_fusion
  184.5 57.7 %psum.7 = f32[3,1536]{1,0:T(4,128)S(1)} all-reduce(f32[3,1536]{1,0:T(4,128)S(1)} %pad_maximum_fusion), channel_id=1, replica_groups=mesh['group'=2,'dp'=8,'fsdp'=2] {'dp','fsdp'}, use_global_device_ids=true, to_apply=%region_10.0 | all-reduce | flops 4608 | bytes 36864 | tf_op jit(solution)/shard_map/psum | solution.py:118
  242.1 0.6 broadcast_multiply_fusion.2
  242.7 0.0 copy-done.1
  (8 shorter events, 0.1 us)
Async XLA Ops:
  7.2 29.9 %copy-start = (bf16[8,64,1536]{2,1,0:T(8,128)(2,1)S(1)}, bf16[8,64,1536]{2,1,0:T(8,128)(2,1)}, u32[]{:S(2)}) copy-start(bf16[8,64,1536]{2,1,0:T(8,128)(2,1)} %param.8) | copy-start | bytes 4718596
  7.2 29.9 %all-gather.3.cloned.1.call-start = ((), (), s32[]{:S(2)}) async-start(), calls=%async_computation.1 | async-start | bytes 14155776 | tf_op jit(solution)/shard_map/all_gather | solution.py:81
  14.0 0.8 copy-start.5
  14.0 1.0 copy-start.7
  14.0 1.1 copy-start.8
  14.0 78.7 %all-gather.5.cloned.1.call-start = ((), (), s32[]{:S(2)}) async-start(), calls=%async_computation.2 | async-start | bytes 14155776 | tf_op jit(solution)/shard_map/all_gather | solution.py:84
  14.8 167.2 %reduce-scatter.2.cloned.1.call-start = ((), (), s32[]{:S(2)}) async-start(), calls=%async_computation.3 | async-start | bytes 835584 | tf_op jit(solution)/shard_map/reduce_scatter | solution.py:107
  70.1 13.4 %copy-start.3 = (f32[8,64,16,96]{3,2,1,0:T(8,128)S(1)}, f32[8,64,16,96]{3,2,1,0:T(8,128)}, u32[]{:S(2)}) copy-start(f32[8,64,16,96]{3,2,1,0:T(8,128)} %reshape_squeeze.7) | copy-start | bytes 9437188
  92.7 3.2 %copy-start.4 = (f32[1536]{0:T(1024)S(1)}, f32[1536]{0:T(1024)}, u32[]{:S(2)}) copy-start(f32[1536]{0:T(1024)} %param.15) | copy-start | bytes 18436
  92.7 3.2 %copy-start.6 = (bf16[8,1536]{1,0:T(8,128)(2,1)S(1)}, bf16[8,1536]{1,0:T(8,128)(2,1)}, u32[]{:S(2)}) copy-start(bf16[8,1536]{1,0:T(8,128)(2,1)} %param.9) | copy-start | bytes 73732
  128.1 10.3 %copy-start.2 = (f32[8,64,16,96]{3,2,1,0:T(8,128)S(1)}, f32[8,64,16,96]{3,2,1,0:T(8,128)}, u32[]{:S(2)}) copy-start(f32[8,64,16,96]{3,2,1,0:T(8,128)} %reshape_squeeze.6) | copy-start | bytes 9437188
  128.1 114.7 %copy-start.1 = (bf16[8,64,1536]{2,1,0:T(8,128)(2,1)S(1)}, bf16[8,64,1536]{2,1,0:T(8,128)(2,1)}, u32[]{:S(2)}) copy-start(bf16[8,64,1536]{2,1,0:T(8,128)(2,1)} %param.8) | copy-start | bytes 4718596
Sparse Core Ops, SparseCore 0:
  14.1 22.9 all-gather.2
  38.7 21.3 all-gather.4
  128.2 53.7 reduce-scatter.1
where the time goes:
time: 250 us; the launch traced here: 249 us
  blocking collectives  80.3 us (32%)
  waiting for transfers between devices  62.3 us (25%)
  matrix products  48.9 us (20%)
  local copies, waits for them, and re-layouts  30.3 us (12%)
  between operations  13.9 us (6%)
  other arithmetic  13.5 us (5%)
    psum x1, blocking collectives, on_device(): lax.psum(jnp.stack([grad_key, grad_value, grad_text]), ('dp', 'fsdp'))  57.7 us
    reduce_scatter x1, waiting for transfers between devices, on_device(): lax.psum_scatter(text_side(coeffs, image_sent), ('dp', 'fsdp'), scatter_d...  39.6 us
    all_gather x1, blocking collectives, on_device(): all_text = lax.all_gather(text_sent, ('dp', 'fsdp'), axis=0, tiled=True)  22.7 us
    all_gather x1, waiting for transfers between devices, on_device(): lax.all_gather(kv_weight, 'fsdp', axis=2, tiled=True)  22 us
    dot_general x1, matrix products, pool_heads(): jnp.einsum('nphe,he->nhp', scaled_keys, probe_heads, precision=HIGHEST)  10.4 us
    dot_general x1, matrix products, key_grad(): jnp.einsum('nphe,nhe->nhp', scaled_values, d_heads, precision=HIGHEST)  10 us
    slice x2, local copies, waits for them, and re-layouts, on_device(): keys_raw = projected[0].reshape(row_count, PATCHES, HEADS, HEAD_SIZE)  8.65 us
    dot_general x1, matrix products, on_device(): jnp.einsum('td,kdc->ktc', flat_tokens, lax.all_gather(kv_weight, 'fsdp',...  7.67 us
  transfers between devices with their start and end apart: 3, of which 2 were waited for; matrix products, arithmetic and copies ran while one was open for 28% of the time, Pallas kernels for 0%

commit v1 on v0

v1 whole, which is shorter than its diff:
```python
import functools
import math

import jax
import jax.numpy as jnp
from jax import lax
from jax.experimental import pallas as pl
from jax.experimental.pallas import tpu as pltpu
from jax.sharding import PartitionSpec as P

HEAD_SIZE = 96
PATCHES = 64
LOGIT_SCALE = 10.0
LOGIT_BIAS = -2.0
EPSILON = 1e-06
MESH = pl.DeviceIdType.MESH
BF16 = jnp.bfloat16
F32 = jnp.float32


def mm(a, b):
    return jnp.dot(a, b, preferred_element_type=F32)


def mm_nt(a, b):
    return lax.dot_general(a, b, (((1,), (1,)), ((), ())), preferred_element_type=F32)


def split(x):
    high = x.astype(BF16)
    low = (x - high.astype(F32)).astype(BF16)
    return jnp.concatenate([high, low], axis=0)


def join(x):
    m = x.shape[0] // 2
    return x[:m] + x[m:]


def per_image(x, op, fill):
    lanes = lax.broadcasted_iota(jnp.int32, (x.shape[0], 128), 1)
    low = lanes < PATCHES
    blocks = []
    for j in range(x.shape[1] // 128):
        b = x[:, 128 * j : 128 * j + 128]
        first = op(jnp.where(low, b, fill), axis=1, keepdims=True)
        second = op(jnp.where(low, fill, b), axis=1, keepdims=True)
        blocks.append(jnp.where(low, first, second))
    return jnp.concatenate(blocks, axis=1)


def sigmoid(x):
    return 1.0 / (1.0 + jnp.exp(-x))


def kernel(
    n_dp, rows, tok_hbm, txt_hbm, kv_hbm, hw_hbm, probe_hbm, sk_hbm, sv_hbm, st_hbm,
    ig_out, tg_out, ia_out,
    tok, kw, vw, hw0, hw1, txt_in, txt, probe, sk, sv, st, tpart, ipart, all_text, all_image,
    att, ctx, fin, local_sem, tok_send, tok_recv, pair_send, pair_recv,
    text_send, text_recv, image_send, image_recv, fin_send, fin_recv,
):
    dp = lax.axis_index("dp")
    f = lax.axis_index("fsdp")
    other = 1 - f
    me = dp * 2 + f
    d_model = tok.shape[2]
    half_d = kw.shape[1]
    heads = half_d // HEAD_SIZE
    pair = 2 * rows
    half_tok = rows * PATCHES
    chunk = half_tok // 2
    n_dev = 2 * n_dp
    count = n_dp * pair

    copies = []

    def load(src, dst):
        c = pltpu.make_async_copy(src, dst, local_sem.at[len(copies)])
        c.start()
        copies.append(c)
        return c

    c_txt = load(txt_hbm, txt_in)
    c_vec = [load(probe_hbm, probe), load(sk_hbm, sk), load(sv_hbm, sv), load(st_hbm, st)]
    c_kw = load(kv_hbm.at[0], kw)
    c_tok = [
        load(tok_hbm.at[pl.ds(chunk * i, chunk)], tok.at[0, pl.ds(chunk * i, chunk)]) for i in range(2)
    ]
    c_hw1 = load(hw_hbm.at[1], hw1)
    c_vw = load(kv_hbm.at[1], vw)
    c_hw0 = load(hw_hbm.at[0], hw0)

    barrier = pltpu.get_barrier_semaphore()

    def greet(k, carry):
        peer = lax.rem(me + k, n_dev)
        pl.semaphore_signal(
            barrier, inc=1, device_id={"dp": peer // 2, "fsdp": lax.rem(peer, 2)}, device_id_type=MESH
        )
        return carry

    lax.fori_loop(1, n_dev, greet, 0)

    c_txt.wait()
    mine = pl.ds(pl.multiple_of(f * rows, rows), rows)
    txt[mine, :] = txt_in[...].astype(F32)

    pl.semaphore_wait(barrier, n_dev - 1)

    def to_partner(src, dst, send, recv):
        return pltpu.make_async_remote_copy(
            src_ref=src, dst_ref=dst, send_sem=send, recv_sem=recv,
            device_id={"fsdp": other}, device_id_type=MESH,
        )

    r_txt = to_partner(txt.at[mine], txt.at[mine], pair_send.at[0], pair_recv.at[0])
    r_txt.start()
    r_tok = []
    for i in range(2):
        r = to_partner(
            tok_hbm.at[pl.ds(chunk * i, chunk)], tok.at[1, pl.ds(chunk * i, chunk)],
            tok_send.at[i], tok_recv.at[i],
        )
        r.start()
        r_tok.append(r)

    def my_half(v):
        return jnp.where(f == 0, v[:, :half_d], v[:, half_d:])

    row_id = lax.broadcasted_iota(jnp.int32, (heads, half_d), 0)
    col_id = lax.broadcasted_iota(jnp.int32, (heads, half_d), 1)
    head_mask = ((col_id >= row_id * HEAD_SIZE) & (col_id < (row_id + 1) * HEAD_SIZE)).astype(F32)

    for c in c_vec:
        c.wait()
    probe_h = my_half(probe[...]) * (1.0 / math.sqrt(HEAD_SIZE))
    sv_h = my_half(sv[...])
    query = head_mask * (probe_h * my_half(sk[...]))
    c_kw.wait()
    query_tok = split(join(mm_nt(split(query), kw[...])))

    group = chunk // PATCHES
    ga = lax.broadcasted_iota(jnp.int32, (group, heads, chunk), 0) * PATCHES
    gb = lax.broadcasted_iota(jnp.int32, (group, heads, chunk), 2)
    block_mask = ((gb >= ga) & (gb < ga + PATCHES)).astype(F32)

    def attend(side, part):
        t = tok[side, part * chunk : (part + 1) * chunk, :]
        scores = join(mm_nt(query_tok, t))
        e = jnp.exp(scores - per_image(scores, jnp.max, -jnp.inf))
        a = e / per_image(e, jnp.sum, 0.0)
        att[side, :, part * chunk : (part + 1) * chunk] = a
        spread = (a[None] * block_mask).reshape(group * heads, chunk)
        mixed = split(join(mm(split(spread), t)))
        m = group * heads
        at = (side * 2 + part) * m
        ctx[0, at : at + m, :] = mixed[:m]
        ctx[1, at : at + m, :] = mixed[m:]

    for i in range(2):
        c_tok[i].wait()
        attend(0, i)

    c_hw1.wait()
    r_txt.wait()
    t_all = txt[...]
    tpart[0] = mm(my_half(t_all).astype(BF16), hw1[...])
    r_tp = to_partner(tpart.at[0], tpart.at[1], pair_send.at[1], pair_recv.at[1])
    r_tp.start()

    r_tok[0].wait()
    attend(1, 0)

    def unit(e):
        inv = lax.rsqrt(jnp.sum(e * e, axis=1, keepdims=True) + EPSILON)
        return e * inv, inv

    def back(u, inv, g):
        return inv * (g - u * jnp.sum(u * g, axis=1, keepdims=True))

    my_rows = pl.ds(pl.multiple_of(dp * pair, pair), pair)

    def gather_copy(buf, at, send, recv, peer):
        return pltpu.make_async_remote_copy(
            src_ref=buf.at[at], dst_ref=buf.at[at], send_sem=send, recv_sem=recv,
            device_id={"dp": peer}, device_id_type=MESH,
        )

    def gather_start(buf, send, recv):
        def body(k, carry):
            peer = lax.rem(dp + k, n_dp)
            gather_copy(buf, my_rows, send.at[peer], recv.at[dp], peer).start()
            return carry

        lax.fori_loop(1, n_dp, body, 0)

    def gather_wait(buf, send, recv):
        def body(k, carry):
            peer = lax.rem(dp + k, n_dp)
            at = pl.ds(pl.multiple_of(peer * pair, pair), pair)
            c = gather_copy(buf, at, send.at[peer], recv.at[peer], peer)
            c.wait_recv()
            c.wait_send()
            return carry

        lax.fori_loop(1, n_dp, body, 0)

    r_tp.wait()
    text_raw = tpart[0] + tpart[1]
    text_unit, text_inv = unit(text_raw * st[...])
    text_sent = text_unit.astype(BF16)
    all_text[my_rows, :] = text_sent
    gather_start(all_text, text_send, text_recv)

    r_tok[1].wait()
    attend(1, 1)

    def swap(x):
        m = x.shape[0] // 2
        return jnp.where(f == 0, x, jnp.concatenate([x[m:], x[:m]], axis=0))

    c_vw.wait()
    n_ctx = pair * heads
    pooled_all = mm(ctx[...].reshape(2 * n_ctx, d_model), vw[...])
    pooled_all = join(pooled_all).reshape(pair, heads, half_d) * head_mask[None]
    pooled_raw = swap(jnp.sum(pooled_all, axis=1))
    pooled = (pooled_raw * sv_h).astype(BF16)
    c_hw0.wait()
    ipart[0] = mm(pooled, hw0[...])
    r_ip = to_partner(ipart.at[0], ipart.at[1], pair_send.at[2], pair_recv.at[2])
    r_ip.start()

    d_row = lax.broadcasted_iota(jnp.int32, (pair, count), 0) + dp * pair
    d_col = lax.broadcasted_iota(jnp.int32, (pair, count), 1)
    diagonal = (d_row == d_col).astype(F32)

    def coefficients(sent, everyone):
        logits = LOGIT_SCALE * mm_nt(sent, everyone) + LOGIT_BIAS
        return (sigmoid(logits) - diagonal).astype(BF16)

    gather_wait(all_text, text_send, text_recv)
    r_ip.wait()
    image_unit, image_inv = unit(ipart[0] + ipart[1])
    image_sent = image_unit.astype(BF16)
    all_image[my_rows, :] = image_sent
    gather_start(all_image, image_send, image_recv)

    image_grad = LOGIT_SCALE * mm(coefficients(image_sent, all_text[...]), all_text[...])
    ig_out[...] = jnp.where(f == 0, image_grad[:rows], image_grad[rows:]).astype(BF16)
    image_back = back(image_unit, image_inv, image_grad).astype(BF16)
    d_pooled = mm_nt(image_back, hw0[...])
    grad_value = jnp.sum(d_pooled * pooled_raw, axis=0, keepdims=True)

    d_local = swap(d_pooled * sv_h)
    d_spread = (d_local[:, None, :] * head_mask[None]).reshape(n_ctx, half_d)
    direction = join(mm_nt(split(d_spread), vw[...]))
    mixed_keys = jnp.zeros((2 * heads, d_model), F32)
    m = group * heads
    for side in range(2):
        for part in range(2):
            at = (side * 2 + part) * m
            t = tok[side, part * chunk : (part + 1) * chunk, :]
            d_att = join(mm_nt(split(direction[at : at + m]), t))
            d_att = jnp.sum(d_att.reshape(group, heads, chunk) * block_mask, axis=0)
            a = att[side, :, part * chunk : (part + 1) * chunk]
            d_scores = a * (d_att - per_image(a * d_att, jnp.sum, 0.0))
            mixed_keys += mm(split(d_scores), t)
    grad_key = join(mm(split(join(mixed_keys)), kw[...]))
    grad_key = probe_h * jnp.sum(grad_key * head_mask, axis=0, keepdims=True)

    gather_wait(all_image, image_send, image_recv)
    text_grad = LOGIT_SCALE * mm(coefficients(text_sent, all_image[...]), all_image[...])
    tg_out[...] = jnp.where(f == 0, text_grad[:rows], text_grad[rows:]).astype(BF16)
    grad_text = my_half(jnp.sum(back(text_unit, text_inv, text_grad) * text_raw, axis=0, keepdims=True))

    totals = jnp.concatenate([grad_key, grad_value, grad_text], axis=0)
    tiles = half_d // 128
    fin[dp, f] = jnp.zeros(fin.shape[2:], F32)
    for j in range(tiles):
        fin[dp, f, 3 * j : 3 * j + 3, :] = totals[:, 128 * j : 128 * j + 128]

    def fin_copy(slot_dp, slot_f, send, recv, peer_dp, peer_f):
        return pltpu.make_async_remote_copy(
            src_ref=fin.at[slot_dp, slot_f], dst_ref=fin.at[slot_dp, slot_f], send_sem=send, recv_sem=recv,
            device_id={"dp": peer_dp, "fsdp": peer_f}, device_id_type=MESH,
        )

    def fin_start(k, carry):
        peer = lax.rem(me + k, n_dev)
        fin_copy(dp, f, fin_send.at[peer], fin_recv.at[me], peer // 2, lax.rem(peer, 2)).start()
        return carry

    def fin_wait(k, carry):
        peer = lax.rem(me + k, n_dev)
        peer_dp, peer_f = peer // 2, lax.rem(peer, 2)
        c = fin_copy(peer_dp, peer_f, fin_send.at[peer], fin_recv.at[peer], peer_dp, peer_f)
        c.wait_recv()
        c.wait_send()
        return carry

    lax.fori_loop(1, n_dev, fin_start, 0)
    lax.fori_loop(1, n_dev, fin_wait, 0)
    for side in range(2):
        total = jnp.sum(fin[:, side], axis=0) * (1.0 / count)
        for j in range(tiles):
            at = side * half_d + 128 * j
            ia_out[:, at : at + 128] = total[3 * j : 3 * j + 3]


def on_device(n_dp, image_tokens, text_features, kv_weight, head_weight, probe, scale_key, scale_value, scale_text):
    rows, patches, d_model = image_tokens.shape
    half_d = kv_weight.shape[2]
    heads = half_d // HEAD_SIZE
    half_tok = rows * patches
    pair = 2 * rows
    count = n_dp * pair
    dma = pltpu.SemaphoreType.DMA
    vec = (1, d_model)
    vmem = pl.BlockSpec(memory_space=pltpu.VMEM)
    return pl.pallas_call(
        functools.partial(kernel, n_dp, rows),
        out_shape=(
            jax.ShapeDtypeStruct((rows, d_model), BF16),
            jax.ShapeDtypeStruct((rows, d_model), BF16),
            jax.ShapeDtypeStruct((3, d_model), F32),
        ),
        in_specs=[pl.BlockSpec(memory_space=pl.ANY)] * 8,
        out_specs=(vmem, vmem, vmem),
        scratch_shapes=[
            pltpu.VMEM((2, half_tok, d_model), BF16),
            pltpu.VMEM((d_model, half_d), BF16),
            pltpu.VMEM((d_model, half_d), BF16),
            pltpu.VMEM((half_d, d_model), BF16),
            pltpu.VMEM((half_d, d_model), BF16),
            pltpu.VMEM((rows, d_model), BF16),
            pltpu.VMEM((pair, d_model), F32),
            pltpu.VMEM(vec, F32),
            pltpu.VMEM(vec, F32),
            pltpu.VMEM(vec, F32),
            pltpu.VMEM(vec, F32),
            pltpu.VMEM((2, pair, d_model), F32),
            pltpu.VMEM((2, pair, d_model), F32),
            pltpu.VMEM((count, d_model), BF16),
            pltpu.VMEM((count, d_model), BF16),
            pltpu.VMEM((2, heads, half_tok), F32),
            pltpu.VMEM((2, pair * heads, d_model), BF16),
            pltpu.VMEM((n_dp, 2, 24, 128), F32),
            dma((11,)),
            dma((2,)),
            dma((2,)),
            dma((3,)),
            dma((3,)),
            dma((n_dp,)),
            dma((n_dp,)),
            dma((n_dp,)),
            dma((n_dp,)),
            dma((2 * n_dp,)),
            dma((2 * n_dp,)),
        ],
        compiler_params=pltpu.CompilerParams(
            collective_id=0, has_side_effects=True, vmem_limit_bytes=56 * 1024 * 1024
        ),
    )(
        image_tokens.reshape(half_tok, d_model), text_features, kv_weight, head_weight,
        probe.reshape(vec), scale_key.reshape(vec), scale_value.reshape(vec), scale_text.reshape(vec),
    )


def solution(mesh):
    in_specs = (
        P(("group", "dp", "fsdp"), None, None),
        P(("group", "dp", "fsdp"), None),
        P(None, None, "fsdp"),
        P(None, "fsdp", None),
        P(),
        P(),
        P(),
        P(),
    )
    out_specs = (
        P(("group", "dp", "fsdp"), None),
        P(("group", "dp", "fsdp"), None),
        P("group", None),
    )
    return jax.shard_map(
        functools.partial(on_device, mesh.shape["dp"]),
        mesh=mesh, in_specs=in_specs, out_specs=out_specs, check_vma=False,
    )
```

time: 250 us -> 48.2 us (0.19)
  blocking collectives: 80.3 us -> 0 us
  waiting for transfers between devices: 62.3 us -> 0 us
  matrix products: 48.9 us -> 0 us
  Pallas kernels: 0 us -> 37.8 us
  local copies, waits for them, and re-layouts: 30.3 us -> 9.23 us
  other arithmetic: 13.5 us -> 0 us
  between operations: 13.9 us -> 0.64 us
    psum x1 -> x0, blocking collectives: 57.7 us -> none  [on_device(): lax.psum(jnp.stack([grad_key, grad_value, grad_text]), ('dp', 'fsdp'))]
    dot_general x11 -> x0, matrix products: 48.9 us -> none  [the longest x1 10.4 us: pool_heads(): jnp.einsum('nphe,he->nhp', scaled_keys, probe_heads, precision=HIGHEST)]
    reduce_scatter x1 -> x0, waiting for transfers between devices: 39.6 us -> none  [on_device(): lax.psum_scatter(text_side(coeffs, image_sent), ('dp', 'fsdp'), scatter_d...]
    pallas_call x0 -> x1, Pallas kernels: none -> 37.8 us  [on_device(): pl.pallas_call(functools.partial(kernel, n_dp, rows), out_shape=(jax.Shap...]
    all_gather x1 -> x0, blocking collectives: 22.7 us -> none  [on_device(): all_text = lax.all_gather(text_sent, ('dp', 'fsdp'), axis=0, tiled=True)]
    all_gather x2 -> x0, waiting for transfers between devices: 22 us -> none  [the longest x1 22 us: on_device(): lax.all_gather(kv_weight, 'fsdp', axis=2, tiled=True)]
    slice x3 -> x0, local copies, waits for them, and re-layouts: 12.2 us -> none  [the longest x2 8.65 us: on_device(): keys_raw = projected[0].reshape(row_count, PATCHES, HEADS, HEAD_SIZE)]
    another operation x4 -> x0, local copies, waits for them, and re-layouts: 10.7 us -> none  [the longest x1 5.52 us: on_device(): keys_raw = projected[0].reshape(row_count, PATCHES, HEADS, HEAD_SIZE)]
  transfers between devices with their start and end apart: 3 -> 0, of which waited for: 2 -> 0; matrix products, arithmetic and copies ran while one was open for 28% -> 0% of each run, Pallas kernels for 0% -> 0%
where the time goes in v1:
time: 48.2 us; the launch traced here: 47.7 us
  Pallas kernels  37.8 us (78%)
  local copies, waits for them, and re-layouts  9.23 us (19%)
  between operations  0.64 us (1%)
    pallas_call x1, Pallas kernels, on_device(): pl.pallas_call(functools.partial(kernel, n_dp, rows), out_shape=(jax.Shap...  37.8 us
    unnamed x3, local copies, waits for them, and re-layouts  4.04 us
    reshape x1, local copies, waits for them, and re-layouts, on_device(): scale_text.reshape(vec)  1.3 us
    reshape x1, local copies, waits for them, and re-layouts, on_device(): probe.reshape(vec)  1.3 us
    reshape x1, local copies, waits for them, and re-layouts, on_device(): scale_value.reshape(vec)  1.29 us
    reshape x1, local copies, waits for them, and re-layouts, on_device(): scale_key.reshape(vec)  1.29 us

profile of v1, /device:TPU:0, one launch (start us, length us, event | category | flops | bytes accessed | tf_op | source)
XLA Modules:
  0.0 47.7 jit_solution(8369679521578174025)
XLA Ops:
  0.6 1.3 %reshape.22.probe_hbm = f32[1,1536]{1,0:T(1,128)} reshape(f32[1536]{0:T(1024)} %param.12) | data formatting | bytes 12288 | tf_op jit(solution)/shard_map/reshape | solution.py:366
  1.9 1.3 %reshape.23.sk_hbm = f32[1,1536]{1,0:T(1,128)} reshape(f32[1536]{0:T(1024)} %param.13) | data formatting | bytes 12288 | tf_op jit(solution)/shard_map/reshape | solution.py:366
  3.2 1.3 %reshape.24.sv_hbm = f32[1,1536]{1,0:T(1,128)} reshape(f32[1536]{0:T(1024)} %param.14) | data formatting | bytes 12288 | tf_op jit(solution)/shard_map/reshape | solution.py:366
  4.5 1.3 %reshape.25.st_hbm = f32[1,1536]{1,0:T(1,128)} reshape(f32[1536]{0:T(1024)} %param.15) | data formatting | bytes 12288 | tf_op jit(solution)/shard_map/reshape | solution.py:366
  5.8 37.8 %shard_map.103 = (bf16[8,1536]{1,0:T(8,128)(2,1)}, bf16[8,1536]{1,0:T(8,128)(2,1)}, f32[3,1536]{1,0:T(4,128)}) custom-call(bf16[512,1536]{1,0:T(8,128)(2,1)} %bitcast.1, bf16[8,1536]{1,0:T(8,128)(2,1)} %txt_hbm.1, bf16[2,1536,768]{2,1,0:T(8,128)(2,1)} %kv_hbm.1, bf16[2,768,1536]{2,1,0:T(8,128)(2,1)} %hw_hbm.1, f32[1,1536]{1,0:T(1,128)} %reshape.22.probe_hbm, ...), custom_call_target="tpu_custom_call" | custom-call | tf_op jit(solution)/shard_map/pallas_call | solution.py:321
  43.7 1.3 %copy.14 = bf16[8,1536]{1,0:T(8,128)(2,1)} copy(bf16[8,1536]{1,0:T(8,128)(2,1)} %get-tuple-element.6) | data formatting | bytes 49152
  45.0 1.3 %copy.15 = bf16[8,1536]{1,0:T(8,128)(2,1)} copy(bf16[8,1536]{1,0:T(8,128)(2,1)} %get-tuple-element.7) | data formatting | bytes 49152
  46.4 1.3 %copy.16 = f32[3,1536]{1,0:T(4,128)} copy(f32[3,1536]{1,0:T(4,128)} %get-tuple-element.8) | data formatting | bytes 36864

commit v2 on v1

v2 whole, which is shorter than its diff:
```python
import functools
import math

import jax
import jax.numpy as jnp
from jax import lax
from jax.experimental import pallas as pl
from jax.experimental.pallas import tpu as pltpu
from jax.sharding import PartitionSpec as P

HEAD_SIZE = 96
PATCHES = 64
LOGIT_SCALE = 10.0
LOGIT_BIAS = -2.0
EPSILON = 1e-06
MESH = pl.DeviceIdType.MESH
BF16 = jnp.bfloat16
F32 = jnp.float32


def row(ref):
    return ref[...].reshape(1, ref.shape[0])


def mm(a, b):
    return jnp.dot(a, b, preferred_element_type=F32)


def mm_nt(a, b):
    return lax.dot_general(a, b, (((1,), (1,)), ((), ())), preferred_element_type=F32)


def split(x):
    high = x.astype(BF16)
    low = (x - high.astype(F32)).astype(BF16)
    return jnp.concatenate([high, low], axis=0)


def join(x):
    m = x.shape[0] // 2
    return x[:m] + x[m:]


def per_image(x, op, fill):
    lanes = lax.broadcasted_iota(jnp.int32, (x.shape[0], 128), 1)
    low = lanes < PATCHES
    blocks = []
    for j in range(x.shape[1] // 128):
        b = x[:, 128 * j : 128 * j + 128]
        first = op(jnp.where(low, b, fill), axis=1, keepdims=True)
        second = op(jnp.where(low, fill, b), axis=1, keepdims=True)
        blocks.append(jnp.where(low, first, second))
    return jnp.concatenate(blocks, axis=1)


def sigmoid(x):
    return 1.0 / (1.0 + jnp.exp(-x))


def kernel(
    n_hi, n_lo, rows, tok_hbm, txt_hbm, kv_hbm, hw_hbm, probe_hbm, sk_hbm, sv_hbm, st_hbm,
    ig_out, tg_out, ia_out,
    tok, kw, vw, hw0, hw1, txt_in, txt, probe, sk, sv, st, tpart, ipart, all_text, all_image,
    att, ctx, fin_hi, fin_lo, local_sem, tok_send, tok_recv, pair_send, pair_recv,
    text_sems, image_sems, fin_hi_send, fin_hi_recv, fin_lo_send, fin_lo_recv,
):
    dp = lax.axis_index("dp")
    f = lax.axis_index("fsdp")
    other = 1 - f
    hi, lo = dp // n_lo, lax.rem(dp, n_lo)
    n_dp = n_hi * n_lo
    square = lo * 2 + f
    d_model = tok.shape[2]
    half_d = kw.shape[1]
    heads = half_d // HEAD_SIZE
    pair = 2 * rows
    half_tok = rows * PATCHES
    chunk = half_tok // 2
    count = n_dp * pair

    copies = []

    def load(src, dst):
        c = pltpu.make_async_copy(src, dst, local_sem.at[len(copies)])
        c.start()
        copies.append(c)
        return c

    c_txt = load(txt_hbm, txt_in)
    c_hw1 = load(hw_hbm.at[1], hw1)
    c_vec = [load(probe_hbm, probe), load(sk_hbm, sk), load(sv_hbm, sv), load(st_hbm, st)]
    c_kw = load(kv_hbm.at[0], kw)
    c_tok = [
        load(tok_hbm.at[pl.ds(chunk * i, chunk)], tok.at[0, pl.ds(chunk * i, chunk)]) for i in range(2)
    ]
    c_vw = load(kv_hbm.at[1], vw)
    c_hw0 = load(hw_hbm.at[0], hw0)

    barrier = pltpu.get_barrier_semaphore()

    def at_hi(k):
        return {"dp": lax.rem(hi + k, n_hi) * n_lo + lo, "fsdp": f}

    def at_square(k):
        peer = lax.rem(square + k, 2 * n_lo)
        return {"dp": hi * n_lo + peer // 2, "fsdp": lax.rem(peer, 2)}

    def greet(where):
        def body(k, carry):
            pl.semaphore_signal(barrier, inc=1, device_id=where(k), device_id_type=MESH)
            return carry

        return body

    lax.fori_loop(1, 2 * n_lo, greet(at_square), 0)
    lax.fori_loop(1, n_hi, greet(at_hi), 0)

    c_txt.wait()
    mine = pl.ds(pl.multiple_of(f * rows, rows), rows)
    txt[mine, :] = txt_in[...].astype(F32)

    pl.semaphore_wait(barrier, 2 * n_lo - 1 + n_hi - 1)

    def to_partner(src, dst, send, recv):
        return pltpu.make_async_remote_copy(
            src_ref=src, dst_ref=dst, send_sem=send, recv_sem=recv,
            device_id={"fsdp": other}, device_id_type=MESH,
        )

    r_txt = to_partner(txt.at[mine], txt.at[mine], pair_send.at[0], pair_recv.at[0])
    r_txt.start()
    r_tok = []
    for i in range(2):
        r = to_partner(
            tok_hbm.at[pl.ds(chunk * i, chunk)], tok.at[1, pl.ds(chunk * i, chunk)],
            tok_send.at[i], tok_recv.at[i],
        )
        r.start()
        r_tok.append(r)

    def my_half(v):
        return jnp.where(f == 0, v[:, :half_d], v[:, half_d:])

    row_id = lax.broadcasted_iota(jnp.int32, (heads, half_d), 0)
    col_id = lax.broadcasted_iota(jnp.int32, (heads, half_d), 1)
    head_mask = ((col_id >= row_id * HEAD_SIZE) & (col_id < (row_id + 1) * HEAD_SIZE)).astype(F32)

    def unit(e):
        inv = lax.rsqrt(jnp.sum(e * e, axis=1, keepdims=True) + EPSILON)
        return e * inv, inv

    def back(u, inv, g):
        return inv * (g - u * jnp.sum(u * g, axis=1, keepdims=True))

    my_rows = pl.ds(pl.multiple_of(dp * pair, pair), pair)

    def gather_copy(buf, side, origin, send, recv, peer, core):
        block = buf.at[side, pl.ds(pl.multiple_of(origin * pair, pair), pair)]
        return pltpu.make_async_remote_copy(
            src_ref=block, dst_ref=block, send_sem=send, recv_sem=recv,
            device_id={"dp": peer, "fsdp": core}, device_id_type=MESH,
        )

    def each(low, high, body):
        def step(k, carry):
            body(k)
            return carry

        lax.fori_loop(low, high, step, 0)

    def gather(buf, sems):
        hi_send, lo_send, recv, core_send, core_recv = sems

        def to_hi(k):
            h = lax.rem(hi + k, n_hi)
            return gather_copy(buf, f, dp, hi_send.at[h], recv.at[dp], h * n_lo + lo, f)

        def to_lo(h, k):
            t = lax.rem(lo + k, n_lo)
            origin = h * n_lo + lo
            return gather_copy(buf, f, origin, lo_send.at[h * n_lo + t], recv.at[origin], hi * n_lo + t, f)

        def to_core(origin):
            return gather_copy(buf, f, origin, core_send.at[origin], core_recv.at[origin], dp, other)

        def arrived(origin):
            gather_copy(buf, f, origin, hi_send.at[0], recv.at[origin], dp, other).wait_recv()

        def start():
            each(1, n_hi, lambda k: to_hi(k).start())
            each(1, n_lo, lambda k: to_lo(hi, k).start())

        def forward_hi():
            def body(k):
                h = lax.rem(hi + k, n_hi)
                arrived(h * n_lo + lo)
                each(1, n_lo, lambda j: to_lo(h, j).start())
                to_core(h * n_lo + lo).start()

            each(1, n_hi, body)

        def forward_lo():
            def body(k):
                def inner(j):
                    origin = lax.rem(hi + j, n_hi) * n_lo + lax.rem(lo + k, n_lo)
                    arrived(origin)
                    to_core(origin).start()

                each(0, n_hi, inner)

            each(1, n_lo, body)

        def finish():
            def cores(k):
                origin = lax.rem(dp + k, n_dp)
                gather_copy(buf, other, origin, core_send.at[origin], core_recv.at[origin], dp, other).wait_recv()

            def sent(k):
                to_core(lax.rem(dp + k, n_dp)).wait_send()

            each(1, n_dp, cores)
            each(1, n_dp, sent)
            each(1, n_hi, lambda k: to_hi(k).wait_send())
            each(0, n_hi, lambda h: each(1, n_lo, lambda k: to_lo(h, k).wait_send()))

        return start, forward_hi, forward_lo, finish

    def place(buf, sent):
        buf[0, my_rows, :] = sent[:, :half_d]
        buf[1, my_rows, :] = sent[:, half_d:]

    def similarity(sent, buf):
        return mm_nt(sent[:, :half_d], buf[0]) + mm_nt(sent[:, half_d:], buf[1])

    def weigh(coeffs, buf):
        return LOGIT_SCALE * jnp.concatenate([mm(coeffs, buf[0]), mm(coeffs, buf[1])], axis=1)

    text_start, text_hi, text_lo, text_finish = gather(all_text, text_sems)
    image_start, image_hi, image_lo, image_finish = gather(all_image, image_sems)

    for c in c_vec:
        c.wait()
    probe_h = my_half(row(probe)) * (1.0 / math.sqrt(HEAD_SIZE))
    sv_h = my_half(row(sv))
    query = head_mask * (probe_h * my_half(row(sk)))
    c_hw1.wait()
    r_txt.wait()
    t_all = txt[...]
    tpart[0] = mm(my_half(t_all).astype(BF16), hw1[...])
    r_tp = to_partner(tpart.at[0], tpart.at[1], pair_send.at[1], pair_recv.at[1])
    r_tp.start()

    c_kw.wait()
    query_tok = split(join(mm_nt(split(query), kw[...])))

    group = chunk // PATCHES
    ga = lax.broadcasted_iota(jnp.int32, (group, heads, chunk), 0) * PATCHES
    gb = lax.broadcasted_iota(jnp.int32, (group, heads, chunk), 2)
    block_mask = ((gb >= ga) & (gb < ga + PATCHES)).astype(F32)

    def attend(side, part):
        t = tok[side, part * chunk : (part + 1) * chunk, :]
        scores = join(mm_nt(query_tok, t))
        e = jnp.exp(scores - per_image(scores, jnp.max, -jnp.inf))
        a = e / per_image(e, jnp.sum, 0.0)
        att[side, :, part * chunk : (part + 1) * chunk] = a
        spread = (a[None] * block_mask).reshape(group * heads, chunk)
        mixed = split(join(mm(split(spread), t)))
        m = group * heads
        at = (side * 2 + part) * m
        ctx[0, at : at + m, :] = mixed[:m]
        ctx[1, at : at + m, :] = mixed[m:]

    c_tok[0].wait()
    attend(0, 0)

    r_tp.wait()
    text_raw = tpart[0] + tpart[1]
    text_unit, text_inv = unit(text_raw * row(st))
    text_sent = text_unit.astype(BF16)
    place(all_text, text_sent)
    text_start()

    c_tok[1].wait()
    attend(0, 1)
    text_hi()
    r_tok[0].wait()
    attend(1, 0)
    text_lo()
    r_tok[1].wait()
    attend(1, 1)

    def swap(x):
        m = x.shape[0] // 2
        return jnp.where(f == 0, x, jnp.concatenate([x[m:], x[:m]], axis=0))

    c_vw.wait()
    n_ctx = pair * heads
    pooled_all = mm(ctx[...].reshape(2 * n_ctx, d_model), vw[...])
    pooled_all = join(pooled_all).reshape(pair, heads, half_d) * head_mask[None]
    pooled_raw = swap(jnp.sum(pooled_all, axis=1))
    pooled = (pooled_raw * sv_h).astype(BF16)
    c_hw0.wait()
    ipart[0] = mm(pooled, hw0[...])
    r_ip = to_partner(ipart.at[0], ipart.at[1], pair_send.at[2], pair_recv.at[2])
    r_ip.start()

    d_row = lax.broadcasted_iota(jnp.int32, (pair, count), 0) + dp * pair
    d_col = lax.broadcasted_iota(jnp.int32, (pair, count), 1)
    diagonal = (d_row == d_col).astype(F32)

    def coefficients(sent, buf):
        logits = LOGIT_SCALE * similarity(sent, buf) + LOGIT_BIAS
        return (sigmoid(logits) - diagonal).astype(BF16)

    text_finish()
    r_ip.wait()
    image_unit, image_inv = unit(ipart[0] + ipart[1])
    image_sent = image_unit.astype(BF16)
    place(all_image, image_sent)
    image_start()

    image_grad = weigh(coefficients(image_sent, all_text), all_text)
    ig_out[...] = jnp.where(f == 0, image_grad[:rows], image_grad[rows:]).astype(BF16)
    image_back = back(image_unit, image_inv, image_grad).astype(BF16)
    d_pooled = mm_nt(image_back, hw0[...])
    grad_value = jnp.sum(d_pooled * pooled_raw, axis=0, keepdims=True)

    image_hi()
    d_local = swap(d_pooled * sv_h)
    d_spread = (d_local[:, None, :] * head_mask[None]).reshape(n_ctx, half_d)
    direction = join(mm_nt(split(d_spread), vw[...]))
    mixed_keys = jnp.zeros((2 * heads, d_model), F32)
    m = group * heads
    for side in range(2):
        for part in range(2):
            at = (side * 2 + part) * m
            t = tok[side, part * chunk : (part + 1) * chunk, :]
            d_att = join(mm_nt(split(direction[at : at + m]), t))
            d_att = jnp.sum(d_att.reshape(group, heads, chunk) * block_mask, axis=0)
            a = att[side, :, part * chunk : (part + 1) * chunk]
            d_scores = a * (d_att - per_image(a * d_att, jnp.sum, 0.0))
            mixed_keys += mm(split(d_scores), t)
    image_lo()
    grad_key = join(mm(split(join(mixed_keys)), kw[...]))
    grad_key = probe_h * jnp.sum(grad_key * head_mask, axis=0, keepdims=True)

    image_finish()
    text_grad = weigh(coefficients(text_sent, all_image), all_image)
    tg_out[...] = jnp.where(f == 0, text_grad[:rows], text_grad[rows:]).astype(BF16)
    grad_text = my_half(jnp.sum(back(text_unit, text_inv, text_grad) * text_raw, axis=0, keepdims=True))

    totals = jnp.concatenate([grad_key, grad_value, grad_text], axis=0)
    tiles = half_d // 128
    fin_hi[hi] = jnp.zeros(fin_hi.shape[1:], F32)
    for j in range(tiles):
        fin_hi[hi, 3 * j : 3 * j + 3, :] = totals[:, 128 * j : 128 * j + 128]

    def send_hi(slot, send, recv, k):
        return pltpu.make_async_remote_copy(
            src_ref=fin_hi.at[slot], dst_ref=fin_hi.at[slot], send_sem=fin_hi_send.at[send],
            recv_sem=fin_hi_recv.at[recv], device_id=at_hi(k), device_id_type=MESH,
        )

    def send_lo(slot, send, recv, k):
        return pltpu.make_async_remote_copy(
            src_ref=fin_lo.at[slot], dst_ref=fin_lo.at[slot], send_sem=fin_lo_send.at[send],
            recv_sem=fin_lo_recv.at[recv], device_id=at_square(k), device_id_type=MESH,
        )

    def wait_hi(k):
        peer = lax.rem(hi + k, n_hi)
        c = send_hi(peer, k, peer, k)
        c.wait_recv()
        c.wait_send()

    def wait_lo(k):
        peer = lax.rem(square + k, 2 * n_lo)
        c = send_lo(peer, k, peer, k)
        c.wait_recv()
        c.wait_send()

    each(1, n_hi, lambda k: send_hi(hi, k, hi, k).start())
    each(1, n_hi, wait_hi)
    fin_lo[square] = jnp.sum(fin_hi[...], axis=0)
    each(1, 2 * n_lo, lambda k: send_lo(square, k, square, k).start())
    each(1, 2 * n_lo, wait_lo)
    for side in range(2):
        total = fin_lo[side]
        for k in range(1, n_lo):
            total = total + fin_lo[2 * k + side]
        total = total * (1.0 / count)
        for j in range(tiles):
            at = side * half_d + 128 * j
            ia_out[:, at : at + 128] = total[3 * j : 3 * j + 3]


def hand_over(ig, tg, ia, ig_out, tg_out, ia_out):
    ig_out[...] = ig[...]
    tg_out[...] = tg[...]
    ia_out[...] = ia[...]


def on_device(n_dp, image_tokens, text_features, kv_weight, head_weight, probe, scale_key, scale_value, scale_text):
    rows, patches, d_model = image_tokens.shape
    half_d = kv_weight.shape[2]
    heads = half_d // HEAD_SIZE
    half_tok = rows * patches
    pair = 2 * rows
    count = n_dp * pair
    n_lo = max(k for k in range(1, n_dp + 1) if n_dp % k == 0 and k * k <= n_dp)
    n_hi = n_dp // n_lo
    dma = pltpu.SemaphoreType.DMA
    vec = (d_model,)
    vmem = pl.BlockSpec(memory_space=pltpu.VMEM)
    out_shape = (
        jax.ShapeDtypeStruct((rows, d_model), BF16),
        jax.ShapeDtypeStruct((rows, d_model), BF16),
        jax.ShapeDtypeStruct((3, d_model), F32),
    )
    results = pl.pallas_call(
        functools.partial(kernel, n_dp // n_lo, n_lo, rows),
        out_shape=out_shape,
        in_specs=[pl.BlockSpec(memory_space=pl.ANY)] * 8,
        out_specs=(vmem, vmem, vmem),
        scratch_shapes=[
            pltpu.VMEM((2, half_tok, d_model), BF16),
            pltpu.VMEM((d_model, half_d), BF16),
            pltpu.VMEM((d_model, half_d), BF16),
            pltpu.VMEM((half_d, d_model), BF16),
            pltpu.VMEM((half_d, d_model), BF16),
            pltpu.VMEM((rows, d_model), BF16),
            pltpu.VMEM((pair, d_model), F32),
            pltpu.VMEM(vec, F32),
            pltpu.VMEM(vec, F32),
            pltpu.VMEM(vec, F32),
            pltpu.VMEM(vec, F32),
            pltpu.VMEM((2, pair, d_model), F32),
            pltpu.VMEM((2, pair, d_model), F32),
            pltpu.VMEM((2, count, half_d), BF16),
            pltpu.VMEM((2, count, half_d), BF16),
            pltpu.VMEM((2, heads, half_tok), F32),
            pltpu.VMEM((2, pair * heads, d_model), BF16),
            pltpu.VMEM((n_hi, 24, 128), F32),
            pltpu.VMEM((2 * n_lo, 24, 128), F32),
            dma((11,)),
            dma((2,)),
            dma((2,)),
            dma((3,)),
            dma((3,)),
            [dma((n_hi,)), dma((n_dp,)), dma((n_dp,)), dma((n_dp,)), dma((n_dp,))],
            [dma((n_hi,)), dma((n_dp,)), dma((n_dp,)), dma((n_dp,)), dma((n_dp,))],
            dma((n_hi,)),
            dma((n_hi,)),
            dma((2 * n_lo,)),
            dma((2 * n_lo,)),
        ],
        compiler_params=pltpu.CompilerParams(
            collective_id=0, has_side_effects=True, vmem_limit_bytes=56 * 1024 * 1024
        ),
    )(
        image_tokens.reshape(half_tok, d_model), text_features, kv_weight, head_weight,
        probe, scale_key, scale_value, scale_text,
    )
    return pl.pallas_call(
        hand_over,
        out_shape=out_shape,
        in_specs=[vmem] * 3,
        out_specs=(vmem, vmem, vmem),
        compiler_params=pltpu.CompilerParams(vmem_limit_bytes=56 * 1024 * 1024),
    )(*results)


def solution(mesh):
    in_specs = (
        P(("group", "dp", "fsdp"), None, None),
        P(("group", "dp", "fsdp"), None),
        P(None, None, "fsdp"),
        P(None, "fsdp", None),
        P(),
        P(),
        P(),
        P(),
    )
    out_specs = (
        P(("group", "dp", "fsdp"), None),
        P(("group", "dp", "fsdp"), None),
        P("group", None),
    )
    return jax.shard_map(
        functools.partial(on_device, mesh.shape["dp"]),
        mesh=mesh, in_specs=in_specs, out_specs=out_specs, check_vma=False,
    )
```

time: 48.2 us -> 39.6 us (0.82)
  local copies, waits for them, and re-layouts: 9.23 us -> 0 us
  Pallas kernels: 37.8 us -> 38.8 us
    reshape x4 -> x0, local copies, waits for them, and re-layouts: 5.19 us -> none  [the longest x1 1.3 us: on_device(): scale_text.reshape(vec)]
    unnamed x3 -> x0, local copies, waits for them, and re-layouts: 4.04 us -> none
    pallas_call x1 -> x2, Pallas kernels: 37.8 us -> 38.8 us  [the longest x1 37.4 us: on_device(): pl.pallas_call(functools.partial(kernel, n_dp // n_lo, n_lo, rows), out_s...]
where the time goes in v2:
time: 39.6 us; the launch traced here: 39.4 us
  Pallas kernels  38.8 us (98%)
  between operations  0.64 us (2%)
    pallas_call x1, Pallas kernels, on_device(): pl.pallas_call(functools.partial(kernel, n_dp // n_lo, n_lo, rows), out_s...  37.4 us
    pallas_call x1, Pallas kernels, on_device(): pl.pallas_call(hand_over, out_shape=out_shape, in_specs=[vmem] * 3, out_s...  1.4 us

profile of v2, /device:TPU:0, one launch (start us, length us, event | category | flops | bytes accessed | tf_op | source)
XLA Modules:
  0.0 39.4 jit_solution(7884863399406001809)
XLA Ops:
  0.6 37.4 %shard_map.103 = (bf16[8,1536]{1,0:T(8,128)(2,1)}, bf16[8,1536]{1,0:T(8,128)(2,1)}, f32[3,1536]{1,0:T(4,128)}) custom-call(bf16[512,1536]{1,0:T(8,128)(2,1)} %bitcast.1, bf16[8,1536]{1,0:T(8,128)(2,1)} %txt_hbm.1, bf16[2,1536,768]{2,1,0:T(8,128)(2,1)} %kv_hbm.1, bf16[2,768,1536]{2,1,0:T(8,128)(2,1)} %hw_hbm.1, f32[1536]{0:T(1024)} %probe_hbm.1, ...), custom_call_target="tpu_custom_call" | custom-call | tf_op jit(solution)/shard_map/pallas_call | solution.py:421
  38.0 1.4 %shard_map.104 = (bf16[8,1536]{1,0:T(8,128)(2,1)}, bf16[8,1536]{1,0:T(8,128)(2,1)}, f32[3,1536]{1,0:T(4,128)}) custom-call(bf16[8,1536]{1,0:T(8,128)(2,1)} %get-tuple-element.6.ig, bf16[8,1536]{1,0:T(8,128)(2,1)} %get-tuple-element.7.tg, f32[3,1536]{1,0:T(4,128)} %get-tuple-element.8.ia), custom_call_target="tpu_custom_call" | custom-call | tf_op jit(solution)/shard_map/pallas_call | solution.py:465

commit v3 on v2

--- a/solution.py
+++ b/solution.py
@@ -61,15 +61,14 @@
     n_hi, n_lo, rows, tok_hbm, txt_hbm, kv_hbm, hw_hbm, probe_hbm, sk_hbm, sv_hbm, st_hbm,
     ig_out, tg_out, ia_out,
     tok, kw, vw, hw0, hw1, txt_in, txt, probe, sk, sv, st, tpart, ipart, all_text, all_image,
-    att, ctx, fin_hi, fin_lo, local_sem, tok_send, tok_recv, pair_send, pair_recv,
-    text_sems, image_sems, fin_hi_send, fin_hi_recv, fin_lo_send, fin_lo_recv,
+    att, ctx, fin_kv, fin_text, local_sem, tok_send, tok_recv, pair_send, pair_recv,
+    text_sems, image_sems, kv_send, kv_recv, ft_send, ft_recv,
 ):
     dp = lax.axis_index("dp")
     f = lax.axis_index("fsdp")
     other = 1 - f
     hi, lo = dp // n_lo, lax.rem(dp, n_lo)
     n_dp = n_hi * n_lo
-    square = lo * 2 + f
     d_model = tok.shape[2]
     half_d = kw.shape[1]
     heads = half_d // HEAD_SIZE
@@ -98,28 +97,30 @@
 
     barrier = pltpu.get_barrier_semaphore()
 
-    def at_hi(k):
-        return {"dp": lax.rem(hi + k, n_hi) * n_lo + lo, "fsdp": f}
-
-    def at_square(k):
-        peer = lax.rem(square + k, 2 * n_lo)
-        return {"dp": hi * n_lo + peer // 2, "fsdp": lax.rem(peer, 2)}
-
-    def greet(where):
-        def body(k, carry):
-            pl.semaphore_signal(barrier, inc=1, device_id=where(k), device_id_type=MESH)
+    me = dp * 2 + f
+    n_dev = 2 * n_dp
+
+    def each(low, high, body):
+        def step(k, carry):
+            body(k)
             return carry
 
-        return body
-
-    lax.fori_loop(1, 2 * n_lo, greet(at_square), 0)
-    lax.fori_loop(1, n_hi, greet(at_hi), 0)
+        lax.fori_loop(low, high, step, 0)
+
+    def device(k):
+        peer = lax.rem(me + k, n_dev)
+        return {"dp": peer // 2, "fsdp": lax.rem(peer, 2)}
+
+    each(
+        1, n_dev,
+        lambda k: pl.semaphore_signal(barrier, inc=1, device_id=device(k), device_id_type=MESH),
+    )
 
     c_txt.wait()
     mine = pl.ds(pl.multiple_of(f * rows, rows), rows)
     txt[mine, :] = txt_in[...].astype(F32)
 
-    pl.semaphore_wait(barrier, 2 * n_lo - 1 + n_hi - 1)
+    pl.semaphore_wait(barrier, n_dev - 1)
 
     def to_partner(src, dst, send, recv):
         return pltpu.make_async_remote_copy(
@@ -160,13 +161,6 @@
             src_ref=block, dst_ref=block, send_sem=send, recv_sem=recv,
             device_id={"dp": peer, "fsdp": core}, device_id_type=MESH,
         )
-
-    def each(low, high, body):
-        def step(k, carry):
-            body(k)
-            return carry
-
-        lax.fori_loop(low, high, step, 0)
 
     def gather(buf, sems):
         hi_send, lo_send, recv, core_send, core_recv = sems
@@ -283,10 +277,8 @@
 
     c_tok[1].wait()
     attend(0, 1)
-    text_hi()
     r_tok[0].wait()
     attend(1, 0)
-    text_lo()
     r_tok[1].wait()
     attend(1, 1)
 
@@ -313,12 +305,14 @@
         logits = LOGIT_SCALE * similarity(sent, buf) + LOGIT_BIAS
         return (sigmoid(logits) - diagonal).astype(BF16)
 
-    text_finish()
+    text_hi()
+    text_lo()
     r_ip.wait()
     image_unit, image_inv = unit(ipart[0] + ipart[1])
     image_sent = image_unit.astype(BF16)
     place(all_image, image_sent)
     image_start()
+    text_finish()
 
     image_grad = weigh(coefficients(image_sent, all_text), all_text)
     ig_out[...] = jnp.where(f == 0, image_grad[:rows], image_grad[rows:]).astype(BF16)
@@ -326,7 +320,6 @@
     d_pooled = mm_nt(image_back, hw0[...])
     grad_value = jnp.sum(d_pooled * pooled_raw, axis=0, keepdims=True)
 
-    image_hi()
     d_local = swap(d_pooled * sv_h)
     d_spread = (d_local[:, None, :] * head_mask[None]).reshape(n_ctx, half_d)
     direction = join(mm_nt(split(d_spread), vw[...]))
@@ -341,58 +334,62 @@
             a = att[side, :, part * chunk : (part + 1) * chunk]
             d_scores = a * (d_att - per_image(a * d_att, jnp.sum, 0.0))
             mixed_keys += mm(split(d_scores), t)
+    image_hi()
     image_lo()
     grad_key = join(mm(split(join(mixed_keys)), kw[...]))
     grad_key = probe_h * jnp.sum(grad_key * head_mask, axis=0, keepdims=True)
+
+    tiles = half_d // 128
+
+    def put(buf, x):
+        buf[me] = jnp.zeros(buf.shape[1:], F32)
+        n = x.shape[0]
+        for j in range(tiles):
+            buf[me, n * j : n * j + n, :] = x[:, 128 * j : 128 * j + 128]
+
+    def total_copy(buf, slot, send, recv, k):
+        return pltpu.make_async_remote_copy(
+            src_ref=buf.at[slot], dst_ref=buf.at[slot], send_sem=send, recv_sem=recv,
+            device_id=device(k), device_id_type=MESH,
+        )
+
+    def total_start(buf, send, recv):
+        each(1, n_dev, lambda k: total_copy(buf, me, send.at[k], recv.at[me], k).start())
+
+    def total_wait(buf, send, recv):
+        def body(k):
+            peer = lax.rem(me + k, n_dev)
+            c = total_copy(buf, peer, send.at[k], recv.at[peer], k)
+            c.wait_recv()
+            c.wait_send()
+
+        each(1, n_dev, body)
+
+    put(fin_kv, jnp.concatenate([grad_key, grad_value], axis=0))
+    total_start(fin_kv, kv_send, kv_recv)
 
     image_finish()
     text_grad = weigh(coefficients(text_sent, all_image), all_image)
     tg_out[...] = jnp.where(f == 0, text_grad[:rows], text_grad[rows:]).astype(BF16)
     grad_text = my_half(jnp.sum(back(text_unit, text_inv, text_grad) * text_raw, axis=0, keepdims=True))
 
-    totals = jnp.concatenate([grad_key, grad_value, grad_text], axis=0)
-    tiles = half_d // 128
-    fin_hi[hi] = jnp.zeros(fin_hi.shape[1:], F32)
-    for j in range(tiles):
-        fin_hi[hi, 3 * j : 3 * j + 3, :] = totals[:, 128 * j : 128 * j + 128]
-
-    def send_hi(slot, send, recv, k):
-        return pltpu.make_async_remote_copy(
-            src_ref=fin_hi.at[slot], dst_ref=fin_hi.at[slot], send_sem=fin_hi_send.at[send],
-            recv_sem=fin_hi_recv.at[recv], device_id=at_hi(k), device_id_type=MESH,
-        )
-
-    def send_lo(slot, send, recv, k):
-        return pltpu.make_async_remote_copy(
-            src_ref=fin_lo.at[slot], dst_ref=fin_lo.at[slot], send_sem=fin_lo_send.at[send],
-            recv_sem=fin_lo_recv.at[recv], device_id=at_square(k), device_id_type=MESH,
-        )
-
-    def wait_hi(k):
-        peer = lax.rem(hi + k, n_hi)
-        c = send_hi(peer, k, peer, k)
-        c.wait_recv()
-        c.wait_send()
-
-    def wait_lo(k):
-        peer = lax.rem(square + k, 2 * n_lo)
-        c = send_lo(peer, k, peer, k)
-        c.wait_recv()
-        c.wait_send()
-
-    each(1, n_hi, lambda k: send_hi(hi, k, hi, k).start())
-    each(1, n_hi, wait_hi)
-    fin_lo[square] = jnp.sum(fin_hi[...], axis=0)
-    each(1, 2 * n_lo, lambda k: send_lo(square, k, square, k).start())
-    each(1, 2 * n_lo, wait_lo)
-    for side in range(2):
-        total = fin_lo[side]
-        for k in range(1, n_lo):
-            total = total + fin_lo[2 * k + side]
-        total = total * (1.0 / count)
-        for j in range(tiles):
-            at = side * half_d + 128 * j
-            ia_out[:, at : at + 128] = total[3 * j : 3 * j + 3]
+    put(fin_text, grad_text)
+    total_start(fin_text, ft_send, ft_recv)
+
+    def write(buf, n, at):
+        for side in range(2):
+            total = buf[side]
+            for k in range(1, n_dp):
+                total = total + buf[2 * k + side]
+            total = total * (1.0 / count)
+            for j in range(tiles):
+                start = side * half_d + 128 * j
+                ia_out[at : at + n, start : start + 128] = total[n * j : n * j + n]
+
+    total_wait(fin_kv, kv_send, kv_recv)
+    write(fin_kv, 2, 0)
+    total_wait(fin_text, ft_send, ft_recv)
+    write(fin_text, 1, 2)
 
 
 def hand_over(ig, tg, ia, ig_out, tg_out, ia_out):
@@ -408,7 +405,8 @@
     half_tok = rows * patches
     pair = 2 * rows
     count = n_dp * pair
-    n_lo = max(k for k in range(1, n_dp + 1) if n_dp % k == 0 and k * k <= n_dp)
+    kv_rows, text_rows = (-(-n * half_d // 1024) * 8 for n in (2, 1))
+    n_lo = 1
     n_hi = n_dp // n_lo
     dma = pltpu.SemaphoreType.DMA
     vec = (d_model,)
@@ -441,8 +439,8 @@
             pltpu.VMEM((2, count, half_d), BF16),
             pltpu.VMEM((2, heads, half_tok), F32),
             pltpu.VMEM((2, pair * heads, d_model), BF16),
-            pltpu.VMEM((n_hi, 24, 128), F32),
-            pltpu.VMEM((2 * n_lo, 24, 128), F32),
+            pltpu.VMEM((2 * n_dp, kv_rows, 128), F32),
+            pltpu.VMEM((2 * n_dp, text_rows, 128), F32),
             dma((11,)),
             dma((2,)),
             dma((2,)),
@@ -450,10 +448,10 @@
             dma((3,)),
             [dma((n_hi,)), dma((n_dp,)), dma((n_dp,)), dma((n_dp,)), dma((n_dp,))],
             [dma((n_hi,)), dma((n_dp,)), dma((n_dp,)), dma((n_dp,)), dma((n_dp,))],
-            dma((n_hi,)),
-            dma((n_hi,)),
-            dma((2 * n_lo,)),
-            dma((2 * n_lo,)),
+            dma((2 * n_dp,)),
+            dma((2 * n_dp,)),
+            dma((2 * n_dp,)),
+            dma((2 * n_dp,)),
         ],
         compiler_params=pltpu.CompilerParams(
             collective_id=0, has_side_effects=True, vmem_limit_bytes=56 * 1024 * 1024

time: 39.6 us -> 33.2 us (0.84)
  Pallas kernels: 38.8 us -> 32.4 us
    pallas_call x1, Pallas kernels: 37.4 us -> 31 us  [on_device(): pl.pallas_call(functools.partial(kernel, n_dp // n_lo, n_lo, rows), out_s...]
where the time goes in v3:
time: 33.2 us; the launch traced here: 33.1 us
  Pallas kernels  32.4 us (98%)
  between operations  0.64 us (2%)
    pallas_call x1, Pallas kernels, on_device(): pl.pallas_call(functools.partial(kernel, n_dp // n_lo, n_lo, rows), out_s...  31 us
    pallas_call x1, Pallas kernels, on_device(): pl.pallas_call(hand_over, out_shape=out_shape, in_specs=[vmem] * 3, out_s...  1.4 us

profile of v3, /device:TPU:0, one launch (start us, length us, event | category | flops | bytes accessed | tf_op | source)
XLA Modules:
  0.0 33.1 jit_solution(5483042430696049958)
XLA Ops:
  0.6 31.0 %shard_map.103 = (bf16[8,1536]{1,0:T(8,128)(2,1)}, bf16[8,1536]{1,0:T(8,128)(2,1)}, f32[3,1536]{1,0:T(4,128)}) custom-call(bf16[512,1536]{1,0:T(8,128)(2,1)} %bitcast.1, bf16[8,1536]{1,0:T(8,128)(2,1)} %txt_hbm.1, bf16[2,1536,768]{2,1,0:T(8,128)(2,1)} %kv_hbm.1, bf16[2,768,1536]{2,1,0:T(8,128)(2,1)} %hw_hbm.1, f32[1536]{0:T(1024)} %probe_hbm.1, ...), custom_call_target="tpu_custom_call" | custom-call | tf_op jit(solution)/shard_map/pallas_call | solution.py:419
  31.7 1.4 %shard_map.104 = (bf16[8,1536]{1,0:T(8,128)(2,1)}, bf16[8,1536]{1,0:T(8,128)(2,1)}, f32[3,1536]{1,0:T(4,128)}) custom-call(bf16[8,1536]{1,0:T(8,128)(2,1)} %get-tuple-element.6.ig, bf16[8,1536]{1,0:T(8,128)(2,1)} %get-tuple-element.7.tg, f32[3,1536]{1,0:T(4,128)} %get-tuple-element.8.ia), custom_call_target="tpu_custom_call" | custom-call | tf_op jit(solution)/shard_map/pallas_call | solution.py:463

commit v4 on v3

--- a/solution.py
+++ b/solution.py
@@ -86,9 +86,9 @@
         return c
 
     c_txt = load(txt_hbm, txt_in)
-    c_hw1 = load(hw_hbm.at[1], hw1)
     c_vec = [load(probe_hbm, probe), load(sk_hbm, sk), load(sv_hbm, sv), load(st_hbm, st)]
     c_kw = load(kv_hbm.at[0], kw)
+    c_hw1 = load(hw_hbm.at[1], hw1)
     c_tok = [
         load(tok_hbm.at[pl.ds(chunk * i, chunk)], tok.at[0, pl.ds(chunk * i, chunk)]) for i in range(2)
     ]
@@ -119,6 +119,21 @@
     c_txt.wait()
     mine = pl.ds(pl.multiple_of(f * rows, rows), rows)
     txt[mine, :] = txt_in[...].astype(F32)
+
+    def my_half(v):
+        return jnp.where(f == 0, v[:, :half_d], v[:, half_d:])
+
+    row_id = lax.broadcasted_iota(jnp.int32, (heads, half_d), 0)
+    col_id = lax.broadcasted_iota(jnp.int32, (heads, half_d), 1)
+    head_mask = ((col_id >= row_id * HEAD_SIZE) & (col_id < (row_id + 1) * HEAD_SIZE)).astype(F32)
+
+    for c in c_vec:
+        c.wait()
+    probe_h = my_half(row(probe)) * (1.0 / math.sqrt(HEAD_SIZE))
+    sv_h = my_half(row(sv))
+    query = head_mask * (probe_h * my_half(row(sk)))
+    c_kw.wait()
+    query_tok = split(join(mm_nt(split(query), kw[...])))
 
     pl.semaphore_wait(barrier, n_dev - 1)
 
@@ -139,13 +154,6 @@
         r.start()
         r_tok.append(r)
 
-    def my_half(v):
-        return jnp.where(f == 0, v[:, :half_d], v[:, half_d:])
-
-    row_id = lax.broadcasted_iota(jnp.int32, (heads, half_d), 0)
-    col_id = lax.broadcasted_iota(jnp.int32, (heads, half_d), 1)
-    head_mask = ((col_id >= row_id * HEAD_SIZE) & (col_id < (row_id + 1) * HEAD_SIZE)).astype(F32)
-
     def unit(e):
         inv = lax.rsqrt(jnp.sum(e * e, axis=1, keepdims=True) + EPSILON)
         return e * inv, inv
@@ -232,11 +240,6 @@
     text_start, text_hi, text_lo, text_finish = gather(all_text, text_sems)
     image_start, image_hi, image_lo, image_finish = gather(all_image, image_sems)
 
-    for c in c_vec:
-        c.wait()
-    probe_h = my_half(row(probe)) * (1.0 / math.sqrt(HEAD_SIZE))
-    sv_h = my_half(row(sv))
-    query = head_mask * (probe_h * my_half(row(sk)))
     c_hw1.wait()
     r_txt.wait()
     t_all = txt[...]
@@ -244,29 +247,27 @@
     r_tp = to_partner(tpart.at[0], tpart.at[1], pair_send.at[1], pair_recv.at[1])
     r_tp.start()
 
-    c_kw.wait()
-    query_tok = split(join(mm_nt(split(query), kw[...])))
-
     group = chunk // PATCHES
     ga = lax.broadcasted_iota(jnp.int32, (group, heads, chunk), 0) * PATCHES
     gb = lax.broadcasted_iota(jnp.int32, (group, heads, chunk), 2)
     block_mask = ((gb >= ga) & (gb < ga + PATCHES)).astype(F32)
 
-    def attend(side, part):
-        t = tok[side, part * chunk : (part + 1) * chunk, :]
-        scores = join(mm_nt(query_tok, t))
+    def attend(side):
+        scores = join(mm_nt(query_tok, tok[side]))
         e = jnp.exp(scores - per_image(scores, jnp.max, -jnp.inf))
         a = e / per_image(e, jnp.sum, 0.0)
-        att[side, :, part * chunk : (part + 1) * chunk] = a
-        spread = (a[None] * block_mask).reshape(group * heads, chunk)
-        mixed = split(join(mm(split(spread), t)))
+        att[side] = a
         m = group * heads
-        at = (side * 2 + part) * m
-        ctx[0, at : at + m, :] = mixed[:m]
-        ctx[1, at : at + m, :] = mixed[m:]
+        for part in range(2):
+            spread = (a[None, :, part * chunk : (part + 1) * chunk] * block_mask).reshape(m, chunk)
+            mixed = split(join(mm(split(spread), tok[side, part * chunk : (part + 1) * chunk, :])))
+            at = (side * 2 + part) * m
+            ctx[0, at : at + m, :] = mixed[:m]
+            ctx[1, at : at + m, :] = mixed[m:]
 
     c_tok[0].wait()
-    attend(0, 0)
+    c_tok[1].wait()
+    attend(0)
 
     r_tp.wait()
     text_raw = tpart[0] + tpart[1]
@@ -275,12 +276,9 @@
     place(all_text, text_sent)
     text_start()
 
-    c_tok[1].wait()
-    attend(0, 1)
     r_tok[0].wait()
-    attend(1, 0)
     r_tok[1].wait()
-    attend(1, 1)
+    attend(1)
 
     def swap(x):
         m = x.shape[0] // 2
@@ -323,17 +321,17 @@
     d_local = swap(d_pooled * sv_h)
     d_spread = (d_local[:, None, :] * head_mask[None]).reshape(n_ctx, half_d)
     direction = join(mm_nt(split(d_spread), vw[...]))
-    mixed_keys = jnp.zeros((2 * heads, d_model), F32)
     m = group * heads
+    blocks = []
     for side in range(2):
         for part in range(2):
             at = (side * 2 + part) * m
-            t = tok[side, part * chunk : (part + 1) * chunk, :]
-            d_att = join(mm_nt(split(direction[at : at + m]), t))
-            d_att = jnp.sum(d_att.reshape(group, heads, chunk) * block_mask, axis=0)
-            a = att[side, :, part * chunk : (part + 1) * chunk]
-            d_scores = a * (d_att - per_image(a * d_att, jnp.sum, 0.0))
-            mixed_keys += mm(split(d_scores), t)
+            d_att = join(mm_nt(split(direction[at : at + m]), tok[side, part * chunk : (part + 1) * chunk, :]))
+            blocks.append(jnp.sum(d_att.reshape(group, heads, chunk) * block_mask, axis=0))
+    d_att = jnp.concatenate(blocks, axis=1)
+    a = jnp.concatenate([att[0], att[1]], axis=1)
+    d_scores = split(a * (d_att - per_image(a * d_att, jnp.sum, 0.0)))
+    mixed_keys = mm(d_scores[:, :half_tok], tok[0]) + mm(d_scores[:, half_tok:], tok[1])
     image_hi()
     image_lo()
     grad_key = join(mm(split(join(mixed_keys)), kw[...]))

time: 33.2 us -> 32.6 us (0.982)
  Pallas kernels: 32.4 us -> 31.8 us
    pallas_call x1, Pallas kernels: 31 us -> 30.4 us  [on_device(): pl.pallas_call(functools.partial(kernel, n_dp // n_lo, n_lo, rows), out_s...]
where the time goes in v4:
time: 32.6 us; the launch traced here: 32.4 us
  Pallas kernels  31.8 us (98%)
  between operations  0.64 us (2%)
    pallas_call x1, Pallas kernels, on_device(): pl.pallas_call(functools.partial(kernel, n_dp // n_lo, n_lo, rows), out_s...  30.4 us
    pallas_call x1, Pallas kernels, on_device(): pl.pallas_call(hand_over, out_shape=out_shape, in_specs=[vmem] * 3, out_s...  1.4 us

profile of v4, /device:TPU:0, one launch (start us, length us, event | category | flops | bytes accessed | tf_op | source)
XLA Modules:
  0.0 32.4 jit_solution(7640900067437812165)
XLA Ops:
  0.6 30.4 %shard_map.103 = (bf16[8,1536]{1,0:T(8,128)(2,1)}, bf16[8,1536]{1,0:T(8,128)(2,1)}, f32[3,1536]{1,0:T(4,128)}) custom-call(bf16[512,1536]{1,0:T(8,128)(2,1)} %bitcast.1, bf16[8,1536]{1,0:T(8,128)(2,1)} %txt_hbm.1, bf16[2,1536,768]{2,1,0:T(8,128)(2,1)} %kv_hbm.1, bf16[2,768,1536]{2,1,0:T(8,128)(2,1)} %hw_hbm.1, f32[1536]{0:T(1024)} %probe_hbm.1, ...), custom_call_target="tpu_custom_call" | custom-call | tf_op jit(solution)/shard_map/pallas_call | solution.py:417
  31.0 1.4 %shard_map.104 = (bf16[8,1536]{1,0:T(8,128)(2,1)}, bf16[8,1536]{1,0:T(8,128)(2,1)}, f32[3,1536]{1,0:T(4,128)}) custom-call(bf16[8,1536]{1,0:T(8,128)(2,1)} %get-tuple-element.6.ig, bf16[8,1536]{1,0:T(8,128)(2,1)} %get-tuple-element.7.tg, f32[3,1536]{1,0:T(4,128)} %get-tuple-element.8.ia), custom_call_target="tpu_custom_call" | custom-call | tf_op jit(solution)/shard_map/pallas_call | solution.py:461

commit v5 on v4

--- a/solution.py
+++ b/solution.py
@@ -61,7 +61,7 @@
     n_hi, n_lo, rows, tok_hbm, txt_hbm, kv_hbm, hw_hbm, probe_hbm, sk_hbm, sv_hbm, st_hbm,
     ig_out, tg_out, ia_out,
     tok, kw, vw, hw0, hw1, txt_in, txt, probe, sk, sv, st, tpart, ipart, all_text, all_image,
-    att, ctx, fin_kv, fin_text, local_sem, tok_send, tok_recv, pair_send, pair_recv,
+    att, ctx, fin_kv, fin_text, last, local_sem, tok_send, tok_recv, pair_send, pair_recv,
     text_sems, image_sems, kv_send, kv_recv, ft_send, ft_recv,
 ):
     dp = lax.axis_index("dp")
@@ -97,8 +97,6 @@
 
     barrier = pltpu.get_barrier_semaphore()
 
-    me = dp * 2 + f
-    n_dev = 2 * n_dp
 
     def each(low, high, body):
         def step(k, carry):
@@ -108,11 +106,11 @@
         lax.fori_loop(low, high, step, 0)
 
     def device(k):
-        peer = lax.rem(me + k, n_dev)
-        return {"dp": peer // 2, "fsdp": lax.rem(peer, 2)}
-
+        return {"dp": lax.rem(dp + k, n_dp), "fsdp": f}
+
+    pl.semaphore_signal(barrier, inc=1, device_id={"fsdp": other}, device_id_type=MESH)
     each(
-        1, n_dev,
+        1, n_dp,
         lambda k: pl.semaphore_signal(barrier, inc=1, device_id=device(k), device_id_type=MESH),
     )
 
@@ -135,7 +133,7 @@
     c_kw.wait()
     query_tok = split(join(mm_nt(split(query), kw[...])))
 
-    pl.semaphore_wait(barrier, n_dev - 1)
+    pl.semaphore_wait(barrier, n_dp)
 
     def to_partner(src, dst, send, recv):
         return pltpu.make_async_remote_copy(
@@ -340,10 +338,10 @@
     tiles = half_d // 128
 
     def put(buf, x):
-        buf[me] = jnp.zeros(buf.shape[1:], F32)
+        buf[dp] = jnp.zeros(buf.shape[1:], F32)
         n = x.shape[0]
         for j in range(tiles):
-            buf[me, n * j : n * j + n, :] = x[:, 128 * j : 128 * j + 128]
+            buf[dp, n * j : n * j + n, :] = x[:, 128 * j : 128 * j + 128]
 
     def total_copy(buf, slot, send, recv, k):
         return pltpu.make_async_remote_copy(
@@ -352,16 +350,16 @@
         )
 
     def total_start(buf, send, recv):
-        each(1, n_dev, lambda k: total_copy(buf, me, send.at[k], recv.at[me], k).start())
+        each(1, n_dp, lambda k: total_copy(buf, dp, send.at[k], recv.at[dp], k).start())
 
     def total_wait(buf, send, recv):
         def body(k):
-            peer = lax.rem(me + k, n_dev)
+            peer = lax.rem(dp + k, n_dp)
             c = total_copy(buf, peer, send.at[k], recv.at[peer], k)
             c.wait_recv()
             c.wait_send()
 
-        each(1, n_dev, body)
+        each(1, n_dp, body)
 
     put(fin_kv, jnp.concatenate([grad_key, grad_value], axis=0))
     total_start(fin_kv, kv_send, kv_recv)
@@ -374,20 +372,19 @@
     put(fin_text, grad_text)
     total_start(fin_text, ft_send, ft_recv)
 
-    def write(buf, n, at):
-        for side in range(2):
-            total = buf[side]
-            for k in range(1, n_dp):
-                total = total + buf[2 * k + side]
-            total = total * (1.0 / count)
-            for j in range(tiles):
-                start = side * half_d + 128 * j
-                ia_out[at : at + n, start : start + 128] = total[n * j : n * j + n]
-
     total_wait(fin_kv, kv_send, kv_recv)
-    write(fin_kv, 2, 0)
+    kv_rows = fin_kv.shape[1]
+    last[f, :kv_rows, :] = jnp.sum(fin_kv[...], axis=0)
     total_wait(fin_text, ft_send, ft_recv)
-    write(fin_text, 1, 2)
+    last[f, kv_rows:, :] = jnp.sum(fin_text[...], axis=0)
+    to_partner(last.at[f], last.at[f], pair_send.at[3], pair_recv.at[3]).start()
+    to_partner(last.at[other], last.at[other], pair_send.at[3], pair_recv.at[3]).wait()
+    for side in range(2):
+        total = last[side] * (1.0 / count)
+        for j in range(tiles):
+            start = side * half_d + 128 * j
+            ia_out[0:2, start : start + 128] = total[2 * j : 2 * j + 2]
+            ia_out[2:3, start : start + 128] = total[kv_rows + j : kv_rows + j + 1]
 
 
 def hand_over(ig, tg, ia, ig_out, tg_out, ia_out):
@@ -437,19 +434,20 @@
             pltpu.VMEM((2, count, half_d), BF16),
             pltpu.VMEM((2, heads, half_tok), F32),
             pltpu.VMEM((2, pair * heads, d_model), BF16),
-            pltpu.VMEM((2 * n_dp, kv_rows, 128), F32),
-            pltpu.VMEM((2 * n_dp, text_rows, 128), F32),
+            pltpu.VMEM((n_dp, kv_rows, 128), F32),
+            pltpu.VMEM((n_dp, text_rows, 128), F32),
+            pltpu.VMEM((2, kv_rows + text_rows, 128), F32),
             dma((11,)),
             dma((2,)),
             dma((2,)),
-            dma((3,)),
-            dma((3,)),
+            dma((4,)),
+            dma((4,)),
             [dma((n_hi,)), dma((n_dp,)), dma((n_dp,)), dma((n_dp,)), dma((n_dp,))],
             [dma((n_hi,)), dma((n_dp,)), dma((n_dp,)), dma((n_dp,)), dma((n_dp,))],
-            dma((2 * n_dp,)),
-            dma((2 * n_dp,)),
-            dma((2 * n_dp,)),
-            dma((2 * n_dp,)),
+            dma((n_dp,)),
+            dma((n_dp,)),
+            dma((n_dp,)),
+            dma((n_dp,)),
         ],
         compiler_params=pltpu.CompilerParams(
             collective_id=0, has_side_effects=True, vmem_limit_bytes=56 * 1024 * 1024

time: 32.6 us -> 32.3 us (level)
  no operation moved by 1% of the time
where the time goes in v5:
time: 32.3 us; the launch traced here: 32.1 us
  Pallas kernels  31.5 us (98%)
  between operations  0.64 us (2%)
    pallas_call x1, Pallas kernels, on_device(): pl.pallas_call(functools.partial(kernel, n_dp // n_lo, n_lo, rows), out_s...  30.1 us
    pallas_call x1, Pallas kernels, on_device(): pl.pallas_call(hand_over, out_shape=out_shape, in_specs=[vmem] * 3, out_s...  1.4 us

profile of v5, /device:TPU:0, one launch (start us, length us, event | category | flops | bytes accessed | tf_op | source)
XLA Modules:
  0.0 32.1 jit_solution(5254828803367348721)
XLA Ops:
  0.6 30.1 %shard_map.103 = (bf16[8,1536]{1,0:T(8,128)(2,1)}, bf16[8,1536]{1,0:T(8,128)(2,1)}, f32[3,1536]{1,0:T(4,128)}) custom-call(bf16[512,1536]{1,0:T(8,128)(2,1)} %bitcast.1, bf16[8,1536]{1,0:T(8,128)(2,1)} %txt_hbm.1, bf16[2,1536,768]{2,1,0:T(8,128)(2,1)} %kv_hbm.1, bf16[2,768,1536]{2,1,0:T(8,128)(2,1)} %hw_hbm.1, f32[1536]{0:T(1024)} %probe_hbm.1, ...), custom_call_target="tpu_custom_call" | custom-call | tf_op jit(solution)/shard_map/pallas_call | solution.py:414
  30.7 1.4 %shard_map.104 = (bf16[8,1536]{1,0:T(8,128)(2,1)}, bf16[8,1536]{1,0:T(8,128)(2,1)}, f32[3,1536]{1,0:T(4,128)}) custom-call(bf16[8,1536]{1,0:T(8,128)(2,1)} %get-tuple-element.6.ig, bf16[8,1536]{1,0:T(8,128)(2,1)} %get-tuple-element.7.tg, f32[3,1536]{1,0:T(4,128)} %get-tuple-element.8.ia), custom_call_target="tpu_custom_call" | custom-call | tf_op jit(solution)/shard_map/pallas_call | solution.py:459
